TPU v7x, 32 devices: a whole 2x2x4 slice. The times are simulated.
32 devices in a mesh: dp: 8 (over z, core), tensor: 4 (over y, x).
Axes of the slice: x: 2, y: 2, z: 4, core: 2. Of those that a mesh axis runs over, the one named last changes fastest.
Arguments:
- tokens: bfloat16 [16384, 1024], P(('dp', 'tensor')), may hold values from -6 to 6
- gain_one: float32 [1024], replicated, may hold values from 0.25 to 1.75
- in_weight: bfloat16 [1024, 3, 1024], P('dp', None, 'tensor'), may hold values from -0.1875 to 0.1875
- conv_weight: float32 [3, 1024], replicated, may hold values from -3 to 3
- out_weight: bfloat16 [1024, 1024], P('tensor', 'dp'), may hold values from -0.1875 to 0.1875
- gain_two: float32 [1024], replicated, may hold values from 0.25 to 1.75
- gate_weight: bfloat16 [1024, 4608], P('dp', 'tensor'), may hold values from -0.1875 to 0.1875
- up_weight: bfloat16 [1024, 4608], P('dp', 'tensor'), may hold values from -0.1875 to 0.1875
- down_weight: bfloat16 [4608, 1024], P('tensor', 'dp'), may hold values from -0.09375 to 0.09375
- out_cotangent: bfloat16 [16384, 1024], P(('dp', 'tensor')), may hold values from -6 to 6
Outputs:
- block_out: bfloat16 [16384, 1024], P(('dp', 'tensor'))
- token_grad: float32 [16384, 1024], P(('dp', 'tensor'))
- gain_one_grad: float32 [1024], replicated
- in_weight_grad: float32 [1024, 3, 1024], P('dp', None, 'tensor')
- conv_weight_grad: float32 [3, 1024], replicated
- out_weight_grad: float32 [1024, 1024], P('tensor', 'dp')
- gain_two_grad: float32 [1024], replicated
- gate_weight_grad: float32 [1024, 4608], P('dp', 'tensor')
- up_weight_grad: float32 [1024, 4608], P('dp', 'tensor')
- down_weight_grad: float32 [4608, 1024], P('tensor', 'dp')
All inputs are finite; a program needn't handle non-finite values.
Results may differ from a plain program's by a relative error of at most 0.017.
Values may be sent and summed in bfloat16 or wider, within the bound.
A program may use at most 192 MiB of HBM per device.

v0:
```python
import jax
import jax.numpy as jnp
from jax import lax
from jax.sharding import PartitionSpec as P

SEQ_LEN = 2048


epsilon = 1e-05


def shifted(array, axis, by):
    length = lax.axis_size(axis)
    pairs = [(i, i + by) for i in range(length) if 0 <= i + by < length]
    return lax.ppermute(array, axis, pairs)


def matmul(former, latter):
    return jnp.dot(former, latter, preferred_element_type=jnp.float32)


def matmul_nt(former, latter):
    return lax.dot_general(
        former, latter, (((1,), (1,)), ((), ())), preferred_element_type=jnp.float32
    )


def matmul_tn(former, latter):
    return lax.dot_general(
        former, latter, (((0,), (0,)), ((), ())), preferred_element_type=jnp.float32
    )


def rms_forward(values, norm_gain):
    inverse_rms = lax.rsqrt(jnp.mean(values * values, axis=-1, keepdims=True) + epsilon)
    return (values * inverse_rms * norm_gain, inverse_rms)


def rms_backward(values, inverse_rms, norm_gain, incoming):
    weighted = incoming * norm_gain
    normed = values * inverse_rms
    gain_grad = jnp.sum(incoming * normed, axis=0)
    values_grad = inverse_rms * (
        weighted - normed * jnp.mean(weighted * normed, axis=-1, keepdims=True)
    )
    return (values_grad, gain_grad)


def project_in(normed_rows, in_matrix):
    row_count = normed_rows.shape[0]
    feature_width = in_matrix.shape[0]
    channels = in_matrix.shape[2]
    projected = matmul(normed_rows, in_matrix.reshape(feature_width, 3 * channels)).reshape(
        row_count, 3, channels
    )
    return (projected[:, 0], projected[:, 1], projected[:, 2])


def conv_forward(gated_input, prior_rows, conv_taps, row_offset):
    row_count = gated_input.shape[0]
    positions = (row_offset + lax.broadcasted_iota(jnp.int32, (row_count, 1), 0)) % SEQ_LEN
    extended = jnp.concatenate([prior_rows, gated_input], axis=0)
    lag_one = jnp.where(positions >= 1, extended[1 : row_count + 1], 0.0)
    lag_two = jnp.where(positions >= 2, extended[0:row_count], 0.0)
    convolved = conv_taps[0] * gated_input + conv_taps[1] * lag_one + conv_taps[2] * lag_two
    return (convolved, lag_one, lag_two)


def finish_mixer(
    grad_conv,
    later_rows,
    conv_taps,
    row_offset,
    gate_b,
    values_x,
    grad_c,
    gated_input,
    lag_one,
    lag_two,
):
    row_count = grad_conv.shape[0]
    channels = grad_conv.shape[1]
    positions = (row_offset + lax.broadcasted_iota(jnp.int32, (row_count + 2, 1), 0)) % SEQ_LEN
    extended = jnp.concatenate([grad_conv, later_rows], axis=0)
    lead_one = jnp.where(positions >= 1, extended, 0.0)[1 : row_count + 1]
    lead_two = jnp.where(positions >= 2, extended, 0.0)[2 : row_count + 2]
    grad_gated = conv_taps[0] * grad_conv + conv_taps[1] * lead_one + conv_taps[2] * lead_two
    grad_proj = jnp.stack([grad_gated * values_x, grad_c, grad_gated * gate_b], axis=1).astype(
        jnp.bfloat16
    )
    tap_grad = jnp.stack(
        [
            jnp.sum(grad_conv * gated_input, axis=0),
            jnp.sum(grad_conv * lag_one, axis=0),
            jnp.sum(grad_conv * lag_two, axis=0),
        ]
    )
    return (grad_proj.reshape(row_count, 3 * channels), tap_grad)


def ffn_front(normed_rows, gate_matrix, up_matrix):
    gate_act = matmul(normed_rows, gate_matrix)
    up_act = matmul(normed_rows, up_matrix)
    hidden = (jax.nn.silu(gate_act) * up_act).astype(jnp.bfloat16)
    return (gate_act, up_act, hidden)


def ffn_back(grad_hidden, gate_act, up_act):
    sigmoid_gate = jax.nn.sigmoid(gate_act)
    grad_gate = (
        grad_hidden * up_act * sigmoid_gate * (1.0 + gate_act * (1.0 - sigmoid_gate))
    ).astype(jnp.bfloat16)
    grad_up = (grad_hidden * (gate_act * sigmoid_gate)).astype(jnp.bfloat16)
    return (grad_gate, grad_up)


def mixer_rows(token_rows, normed_low, conv_weight, in_part, out_part):
    row_count = token_rows.shape[0]
    feature_width = token_rows.shape[1]
    in_full, out_full = (
        lax.all_gather(in_part, "tensor", axis=2, tiled=True),
        lax.all_gather(out_part, "tensor", axis=0, tiled=True),
    )
    row_offset = lax.axis_index("tensor") * row_count
    gate_b, gate_c, values_x = project_in(normed_low, in_full)
    gated_input = gate_b * values_x
    prior_rows = shifted(gated_input[row_count - 2 :], "tensor", 1)
    convolved, lag_one, lag_two = conv_forward(gated_input, prior_rows, conv_weight, row_offset)
    mixer_low = (gate_c * convolved).astype(jnp.bfloat16)
    residual = token_rows + matmul(mixer_low, out_full)

    def backward(grad_resid):
        resid_low = grad_resid.astype(jnp.bfloat16)
        grad_mixer = matmul_nt(resid_low, out_full)
        out_grad = matmul_tn(mixer_low, resid_low)
        grad_conv = grad_mixer * gate_c
        later_rows = shifted(grad_conv[0:2], "tensor", -1)
        grad_proj, tap_full = finish_mixer(
            grad_conv,
            later_rows,
            conv_weight,
            row_offset,
            gate_b,
            values_x,
            grad_mixer * convolved,
            gated_input,
            lag_one,
            lag_two,
        )
        grad_one = matmul_nt(grad_proj, in_full.reshape(feature_width, 3 * feature_width))
        in_grad = matmul_tn(normed_low, grad_proj).reshape(feature_width, 3, feature_width)
        in_share, out_share = (
            lax.psum_scatter(
                in_grad.astype(jnp.bfloat16), "tensor", scatter_dimension=2, tiled=True
            ).astype(jnp.float32),
            lax.psum_scatter(
                out_grad.astype(jnp.bfloat16), "tensor", scatter_dimension=0, tiled=True
            ).astype(jnp.float32),
        )
        return (grad_one, tap_full, in_share, out_share)

    return (residual, backward)


def ffn_rows(residual, gain_two, out_cotangent, gate_part, up_part, down_part):
    gate_full, up_full, down_full = (
        lax.all_gather(gate_part, "tensor", axis=1, tiled=True),
        lax.all_gather(up_part, "tensor", axis=1, tiled=True),
        lax.all_gather(down_part, "tensor", axis=0, tiled=True),
    )
    normed_two, inverse_two = rms_forward(residual, gain_two)
    normed_low_two = normed_two.astype(jnp.bfloat16)
    gate_act, up_act, hidden = ffn_front(normed_low_two, gate_full, up_full)
    block_out = (residual + matmul(hidden, down_full)).astype(jnp.bfloat16)
    grad_hidden = matmul_nt(out_cotangent, down_full)
    down_grad = matmul_tn(hidden, out_cotangent)
    grad_gate, grad_up = ffn_back(grad_hidden, gate_act, up_act)
    grad_two = matmul_nt(grad_gate, gate_full) + matmul_nt(grad_up, up_full)
    gate_grad = matmul_tn(normed_low_two, grad_gate)
    up_grad = matmul_tn(normed_low_two, grad_up)
    branch_grad, gain_two_grad = rms_backward(residual, inverse_two, gain_two, grad_two)
    grad_resid = out_cotangent.astype(jnp.float32) + branch_grad
    gate_share, up_share, down_share = (
        lax.psum_scatter(
            gate_grad.astype(jnp.bfloat16), "tensor", scatter_dimension=1, tiled=True
        ).astype(jnp.float32),
        lax.psum_scatter(
            up_grad.astype(jnp.bfloat16), "tensor", scatter_dimension=1, tiled=True
        ).astype(jnp.float32),
        lax.psum_scatter(
            down_grad.astype(jnp.bfloat16), "tensor", scatter_dimension=0, tiled=True
        ).astype(jnp.float32),
    )
    return (block_out, grad_resid, gain_two_grad, gate_share, up_share, down_share)


def local(
    tokens,
    gain_one,
    in_weight,
    conv_weight,
    out_weight,
    gain_two,
    gate_weight,
    up_weight,
    down_weight,
    out_cotangent,
):
    token_rows = tokens.astype(jnp.float32)
    normed_one, inverse_one = rms_forward(token_rows, gain_one)
    normed_low = normed_one.astype(jnp.bfloat16)
    in_part, out_part, gate_part, up_part, down_part = (
        lax.all_gather(in_weight, "dp", axis=0, tiled=True),
        lax.all_gather(out_weight, "dp", axis=1, tiled=True),
        lax.all_gather(gate_weight, "dp", axis=0, tiled=True),
        lax.all_gather(up_weight, "dp", axis=0, tiled=True),
        lax.all_gather(down_weight, "dp", axis=1, tiled=True),
    )
    residual, mixer_back = mixer_rows(token_rows, normed_low, conv_weight, in_part, out_part)
    ffn_result = ffn_rows(residual, gain_two, out_cotangent, gate_part, up_part, down_part)
    block_out, grad_resid, gain_two_grad, gate_grad, up_grad, down_grad = ffn_result
    grad_one, tap_full, in_grad, out_grad = mixer_back(grad_resid)
    weight_grads = (
        lax.psum_scatter(
            in_grad.astype(jnp.bfloat16), "dp", scatter_dimension=0, tiled=True
        ).astype(jnp.float32),
        lax.psum_scatter(
            out_grad.astype(jnp.bfloat16), "dp", scatter_dimension=1, tiled=True
        ).astype(jnp.float32),
        lax.psum_scatter(
            gate_grad.astype(jnp.bfloat16), "dp", scatter_dimension=0, tiled=True
        ).astype(jnp.float32),
        lax.psum_scatter(
            up_grad.astype(jnp.bfloat16), "dp", scatter_dimension=0, tiled=True
        ).astype(jnp.float32),
        lax.psum_scatter(
            down_grad.astype(jnp.bfloat16), "dp", scatter_dimension=1, tiled=True
        ).astype(jnp.float32),
    )
    norm_grad, gain_one_grad = rms_backward(token_rows, inverse_one, gain_one, grad_one)
    token_grad = grad_resid + norm_grad
    gain_one_sum, gain_two_sum, conv_sum = lax.psum(
        (gain_one_grad, gain_two_grad, tap_full), ("dp", "tensor")
    )
    return (
        block_out,
        token_grad,
        gain_one_sum,
        weight_grads[0],
        conv_sum,
        weight_grads[1],
        gain_two_sum,
        weight_grads[2],
        weight_grads[3],
        weight_grads[4],
    )


def solution(mesh):
    return jax.shard_map(
        local,
        mesh=mesh,
        in_specs=(
            P(("dp", "tensor"), None),
            P(),
            P("dp", None, "tensor"),
            P(),
            P("tensor", "dp"),
            P(),
            P("dp", "tensor"),
            P("dp", "tensor"),
            P("tensor", "dp"),
            P(("dp", "tensor"), None),
        ),
        out_specs=(
            P(("dp", "tensor"), None),
            P(("dp", "tensor"), None),
            P(),
            P("dp", None, "tensor"),
            P(),
            P("tensor", "dp"),
            P(),
            P("dp", "tensor"),
            P("dp", "tensor"),
            P("tensor", "dp"),
        ),
        check_vma=False,
    )
```

profile of v0, /device:TPU:0, one launch (start us, length us, event | category | flops | bytes accessed | tf_op | source)
XLA Modules:
  0.0 1172.5 jit_solution(5057596747168249051)
XLA Ops:
  10.0 27.4 %all-gather.10.cloned.1.call-done = bf16[1024,3,256]{2,0,1:T(8,128)(2,1)} async-done(((bf16[128,3,256]{2,0,1:T(8,128)(2,1)}), bf16[1024,3,256]{2,0,1:T(8,128)(2,1)}) %all-gather.10.cloned.1.call-update) | async-done | bytes 1572880 | tf_op jit(solution)/shard_map/all_gather | solution.py:213
  37.5 14.8 %all_gather.32 = bf16[256,1024]{1,0:T(8,128)(2,1)} all-gather(bf16[256,128]{1,0:T(8,128)(2,1)S(1)} %copy-done.20), channel_id=1, replica_groups=mesh['dp'=8,'tensor'=4] {'dp'}, dimensions={1}, use_global_device_ids=true | all-gather | bytes 589824 | tf_op jit(solution)/shard_map/all_gather | solution.py:214
  52.4 18.8 %all-gather.16.cloned.1.call-done = bf16[1024,1152]{1,0:T(8,128)(2,1)} async-done(((bf16[128,1152]{1,0:T(8,128)(2,1)}), bf16[1024,1152]{1,0:T(8,128)(2,1)}) %all-gather.16.cloned.1.call-update) | async-done | bytes 2359312 | tf_op jit(solution)/shard_map/all_gather | solution.py:215
  71.2 32.1 %all-gather.20.cloned.1.call-done = bf16[1024,1152]{1,0:T(8,128)(2,1)} async-done(((bf16[128,1152]{1,0:T(8,128)(2,1)}), bf16[1024,1152]{1,0:T(8,128)(2,1)}) %all-gather.20.cloned.1.call-update) | async-done | bytes 2359312 | tf_op jit(solution)/shard_map/all_gather | solution.py:216
  103.4 33.3 %all-gather.24.cloned.1.call-done = bf16[1152,1024]{1,0:T(8,128)(2,1)} async-done(((bf16[1152,128]{1,0:T(8,128)(2,1)}), bf16[1152,1024]{1,0:T(8,128)(2,1)}) %all-gather.24.cloned.1.call-update) | async-done | bytes 2359312 | tf_op jit(solution)/shard_map/all_gather | solution.py:217
  137.1 70.0 %all-gather.12.cloned.1.call-done = bf16[1024,3,1024]{2,0,1:T(8,128)(2,1)} async-done(((bf16[1024,3,256]{2,0,1:T(8,128)(2,1)}), bf16[1024,3,1024]{2,0,1:T(8,128)(2,1)}) %all-gather.12.cloned.1.call-update) | async-done | bytes 6291472 | tf_op jit(solution)/shard_map/all_gather | solution.py:121
  229.3 14.9 %all-gather.14.cloned.1.call-done = bf16[1024,1024]{1,0:T(8,128)(2,1)} async-done(((bf16[256,1024]{1,0:T(8,128)(2,1)}), bf16[1024,1024]{1,0:T(8,128)(2,1)}) %all-gather.14.cloned.1.call-update) | async-done | bytes 2097168 | tf_op jit(solution)/shard_map/all_gather | solution.py:122
  247.8 94.7 %all-gather.18.cloned.1.call-done = bf16[1024,4608]{1,0:T(8,128)(2,1)} async-done(((bf16[1024,1152]{1,0:T(8,128)(2,1)}), bf16[1024,4608]{1,0:T(8,128)(2,1)}) %all-gather.18.cloned.1.call-update) | async-done | bytes 9437200 | tf_op jit(solution)/shard_map/all_gather | solution.py:167
  342.4 11.4 fusion.41
  353.8 86.8 %all-gather.22.cloned.1.call-done = bf16[1024,4608]{1,0:T(8,128)(2,1)} async-done(((bf16[1024,1152]{1,0:T(8,128)(2,1)}), bf16[1024,4608]{1,0:T(8,128)(2,1)}) %all-gather.22.cloned.1.call-update) | async-done | bytes 9437200 | tf_op jit(solution)/shard_map/all_gather | solution.py:168
  440.6 11.4 fusion.42
  452.0 86.8 %all-gather.26.cloned.1.call-done = bf16[4608,1024]{1,0:T(8,128)(2,1)} async-done(((bf16[1152,1024]{1,0:T(8,128)(2,1)}), bf16[4608,1024]{1,0:T(8,128)(2,1)}) %all-gather.26.cloned.1.call-update) | async-done | bytes 9437200 | tf_op jit(solution)/shard_map/all_gather | solution.py:169
  538.8 18.0 %multiply_convert_fusion = (bf16[512,4608]{1,0:T(8,128)(2,1)}, bf16[512,4608]{1,0:T(8,128)(2,1)}, bf16[512,4608]{1,0:T(8,128)(2,1)}) fusion(f32[512,4608]{1,0:T(8,128)} %fusion.41, f32[512,4608]{1,0:T(8,128)} %fusion.42, bf16[512,1024]{1,0:T(8,128)(2,1)} %param.19, bf16[4608,1024]{1,0:T(8,128)(2,1)} %all-gather.26.cloned.1.call-done), kind=kOutput, calls=%fused_computation.3 | convolution fusion | flops 4867227648 | bytes 43515904 | tf_op jit(solution)/shard_map/dot_general | solution.py:23
  608.6 10.2 convolution_convert_fusion
  629.9 12.8 %copy.31 = bf16[1024,4608]{0,1:T(8,128)(2,1)} copy(bf16[1024,4608]{1,0:T(8,128)(2,1)} %convolution_convert_fusion.2) | data formatting | bytes 18874368
  652.6 12.7 %copy.33 = bf16[1024,4608]{0,1:T(8,128)(2,1)} copy(bf16[1024,4608]{1,0:T(8,128)(2,1)} %convolution_convert_fusion.1) | data formatting | bytes 18874368
  667.5 20.5 %reduce-scatter.19.cloned.1.call-done = bf16[1024,3,256]{2,0,1:T(8,128)(2,1)} async-done(((bf16[1024,3,1024]{2,0,1:T(8,128)(2,1)}), bf16[1024,3,256]{2,0,1:T(8,128)(2,1)}) %reduce-scatter.19.cloned.1.call-update) | async-done | bytes 1572880 | tf_op jit(solution)/shard_map/reduce_scatter | solution.py:153
  688.1 98.2 %reduce-scatter.29.cloned.1.call-done = bf16[1152,1024]{1,0:T(8,128)(2,1)} async-done(((bf16[4608,1024]{1,0:T(8,128)(2,1)}), bf16[1152,1024]{1,0:T(8,128)(2,1)}) %reduce-scatter.29.cloned.1.call-update) | async-done | bytes 2359312 | tf_op jit(solution)/shard_map/reduce_scatter | solution.py:190
  790.8 94.0 %reduce-scatter.33.cloned.1.call-done = bf16[1152,1024]{1,0:T(8,128)(2,1)} async-done(((bf16[4608,1024]{1,0:T(8,128)(2,1)}), bf16[1152,1024]{1,0:T(8,128)(2,1)}) %reduce-scatter.33.cloned.1.call-update) | async-done | bytes 2359312
  889.2 93.9 %reduce-scatter.35.cloned.1.call-done = bf16[1152,1024]{1,0:T(8,128)(2,1)} async-done(((bf16[4608,1024]{1,0:T(8,128)(2,1)}), bf16[1152,1024]{1,0:T(8,128)(2,1)}) %reduce-scatter.35.cloned.1.call-update) | async-done | bytes 2359312
  1007.1 40.6 %all-reduce = (f32[1024]{0:T(1024)}, f32[3,1024]{1,0:T(4,128)}, f32[1024]{0:T(1024)}) all-reduce(f32[1024]{0:T(1024)S(1)} %get-tuple-element.15, f32[3,1024]{1,0:T(4,128)S(1)} %pad_maximum_fusion.2, f32[1024]{0:T(1024)S(1)} %get-tuple-element.12), channel_id=1, replica_groups=mesh['dp'=8,'tensor'=4] {'dp','tensor'}, use_global_device_ids=true, to_apply=%region_5.6 | all-reduce | flops 5120 | bytes 40960 | tf_op jit(solution)/shard_map/psum | solution.py:242
  1054.5 34.0 %reduce-scatter.37.cloned.1.call-done = bf16[128,1152]{1,0:T(8,128)(2,1)} async-done(((bf16[1024,1152]{1,0:T(8,128)(2,1)}), bf16[128,1152]{1,0:T(8,128)(2,1)}) %reduce-scatter.37.cloned.1.call-update) | async-done | bytes 294928
  1090.5 35.6 %reduce-scatter.25.cloned.1.call-done = bf16[128,1152]{1,0:T(8,128)(2,1)} async-done(((bf16[1024,1152]{1,0:T(8,128)(2,1)}), bf16[128,1152]{1,0:T(8,128)(2,1)}) %reduce-scatter.25.cloned.1.call-update) | async-done | bytes 294928 | tf_op jit(solution)/shard_map/reduce_scatter | solution.py:230
  1127.9 36.0 %reduce-scatter.27.cloned.1.call-done = bf16[128,1152]{1,0:T(8,128)(2,1)} async-done(((bf16[1024,1152]{1,0:T(8,128)(2,1)}), bf16[128,1152]{1,0:T(8,128)(2,1)}) %reduce-scatter.27.cloned.1.call-update) | async-done | bytes 294928 | tf_op jit(solution)/shard_map/reduce_scatter | solution.py:233
  (146 shorter events, 149.0 us)
Async XLA Ops:
  7.2 30.2 %all-gather.10.cloned.1.call-start = ((), (), s32[]{:S(2)}) async-start(), calls=%async_computation.10 | async-start | bytes 1769472 | tf_op jit(solution)/shard_map/all_gather | solution.py:213
  7.9 63.2 %all-gather.16.cloned.1.call-start = ((), (), s32[]{:S(2)}) async-start(), calls=%async_computation.13 | async-start | bytes 2654208 | tf_op jit(solution)/shard_map/all_gather | solution.py:215
  8.7 94.6 %all-gather.20.cloned.1.call-start = ((), (), s32[]{:S(2)}) async-start(), calls=%async_computation.15 | async-start | bytes 2654208 | tf_op jit(solution)/shard_map/all_gather | solution.py:216
  9.4 127.3 %all-gather.24.cloned.1.call-start = ((), (), s32[]{:S(2)}) async-start(), calls=%async_computation.17 | async-start | bytes 2654208 | tf_op jit(solution)/shard_map/all_gather | solution.py:217
  10.0 197.2 %all-gather.12.cloned.1.call-start = ((), (), s32[]{:S(2)}) async-start(), calls=%async_computation.11 | async-start | bytes 7864320 | tf_op jit(solution)/shard_map/all_gather | solution.py:121
  37.4 206.8 %all-gather.14.cloned.1.call-start = ((), (), s32[]{:S(2)}) async-start(), calls=%async_computation.12 | async-start | bytes 2621440 | tf_op jit(solution)/shard_map/all_gather | solution.py:122
  52.3 290.1 %all-gather.18.cloned.1.call-start = ((), (), s32[]{:S(2)}) async-start(), calls=%async_computation.14 | async-start | bytes 11796480 | tf_op jit(solution)/shard_map/all_gather | solution.py:167
  71.2 369.5 %all-gather.22.cloned.1.call-start = ((), (), s32[]{:S(2)}) async-start(), calls=%async_computation.16 | async-start | bytes 11796480 | tf_op jit(solution)/shard_map/all_gather | solution.py:168
  103.3 435.5 %all-gather.26.cloned.1.call-start = ((), (), s32[]{:S(2)}) async-start(), calls=%async_computation.18 | async-start | bytes 11796480 | tf_op jit(solution)/shard_map/all_gather | solution.py:169
  136.7 528.7 %reduce-scatter.23.cloned.1.call-start = ((), (), s32[]{:S(2)}) async-start(), calls=%async_computation.21 | async-start | bytes 2621440 | tf_op jit(solution)/shard_map/reduce_scatter | solution.py:156
  137.1 78.7 %copy-start.23 = (f32[1024]{0:T(1024)S(1)}, f32[1024]{0:T(1024)}, u32[]{:S(2)}) copy-start(f32[1024]{0:T(1024)} %param.11) | copy-start | bytes 12292
  222.2 4.7 collective-permute-start
  247.5 326.9 %copy-start.3 = (f32[512,1024]{1,0:T(8,128)}, f32[512,1024]{1,0:T(8,128)S(1)}, u32[]{:S(2)}) copy-start(f32[512,1024]{1,0:T(8,128)S(1)} %get-tuple-element.32) | copy-start | bytes 6291460
  247.8 192.9 %copy-start.16 = (bf16[512,1024]{1,0:T(8,128)(2,1)}, bf16[512,1024]{1,0:T(8,128)(2,1)S(1)}, u32[]{:S(2)}) copy-start(bf16[512,1024]{1,0:T(8,128)(2,1)S(1)} %multiply_convert_fusion.3) | copy-start | bytes 3145732
  579.0 109.0 %reduce-scatter.19.cloned.1.call-start = ((), (), s32[]{:S(2)}) async-start(), calls=%async_computation.19 | async-start | bytes 7864320 | tf_op jit(solution)/shard_map/reduce_scatter | solution.py:153
  586.0 5.7 collective-permute-start.1
  607.4 178.9 %reduce-scatter.29.cloned.1.call-start = ((), (), s32[]{:S(2)}) async-start(), calls=%async_computation.24 | async-start | bytes 11796480 | tf_op jit(solution)/shard_map/reduce_scatter | solution.py:190
  618.8 265.9 %reduce-scatter.33.cloned.1.call-start = ((), (), s32[]{:S(2)}) async-start(), calls=%async_computation.26 | async-start | bytes 11796480
  642.7 340.4 %reduce-scatter.35.cloned.1.call-start = ((), (), s32[]{:S(2)}) async-start(), calls=%async_computation.27 | async-start | bytes 11796480
  665.4 385.8 %reduce-scatter.31.cloned.1.call-start = ((), (), s32[]{:S(2)}) async-start(), calls=%async_computation.25 | async-start | bytes 589824
  667.5 385.3 %reduce-scatter.21.cloned.1.call-start = ((), (), s32[]{:S(2)}) async-start(), calls=%async_computation.20 | async-start | bytes 1769472 | tf_op jit(solution)/shard_map/reduce_scatter | solution.py:224
  688.0 400.5 %reduce-scatter.37.cloned.1.call-start = ((), (), s32[]{:S(2)}) async-start(), calls=%async_computation.28 | async-start | bytes 2654208
  790.7 335.4 %reduce-scatter.25.cloned.1.call-start = ((), (), s32[]{:S(2)}) async-start(), calls=%async_computation.22 | async-start | bytes 2654208 | tf_op jit(solution)/shard_map/reduce_scatter | solution.py:230
  889.1 274.8 %reduce-scatter.27.cloned.1.call-start = ((), (), s32[]{:S(2)}) async-start(), calls=%async_computation.23 | async-start | bytes 2654208 | tf_op jit(solution)/shard_map/reduce_scatter | solution.py:233
  (24 other events, 268.7 us)
Sparse Core Ops, SparseCore 0:
  9.6 27.7 all-gather.9
  39.0 32.0 all-gather.15
  72.8 30.4 all-gather.19
  104.7 31.9 all-gather.23
  138.4 68.7 all-gather.11
  208.8 35.3 all-gather.13
  246.0 96.3 all-gather.17
  344.3 96.3 all-gather.21
  442.5 96.3 all-gather.25
  579.1 35.3 reduce-scatter.22
  617.8 70.1 reduce-scatter.18
  691.3 95.0 reduce-scatter.28
  789.7 95.0 reduce-scatter.32
  888.0 95.0 reduce-scatter.34
  985.9 30.9 reduce-scatter.30
  1019.0 32.2 reduce-scatter.20
  1053.5 34.9 reduce-scatter.36
  1090.7 35.3 reduce-scatter.24
  1128.4 35.4 reduce-scatter.26
where the time goes:
time: 1180 us; the launch traced here: 1170 us
  waiting for transfers between devices  885 us (75%)
  matrix products  133 us (11%)
  local copies, waits for them, and re-layouts  61 us (5%)
  blocking collectives  55.4 us (5%)
  other arithmetic  17.9 us (2%)
  between operations  14.7 us (1%)
    unnamed x23, waiting for transfers between devices  225 us
    reduce_scatter x1, waiting for transfers between devices, ffn_rows(): lax.psum_scatter(down_grad.astype(jnp.bfloat16), 'tensor', scatter_dimens...  98.2 us
    all_gather x1, waiting for transfers between devices, ffn_rows(): lax.all_gather(gate_part, 'tensor', axis=1, tiled=True)  94.7 us
    all_gather x1, waiting for transfers between devices, ffn_rows(): lax.all_gather(up_part, 'tensor', axis=1, tiled=True)  86.8 us
    all_gather x1, waiting for transfers between devices, ffn_rows(): lax.all_gather(down_part, 'tensor', axis=0, tiled=True)  86.8 us
    all_gather x1, waiting for transfers between devices, mixer_rows(): lax.all_gather(in_part, 'tensor', axis=2, tiled=True)  70 us
    dot_general x5, matrix products, matmul_nt(): lax.dot_general(former, latter, (((1,), (1,)), ((), ())), preferred_eleme...  50.1 us
    unnamed x62, local copies, waits for them, and re-layouts  49.2 us
  transfers between devices with their start and end apart: 21, of which 18 were waited for; matrix products, arithmetic and copies ran while one was open for 14% of the time, Pallas kernels for 0%

commit v1 on v0

v1 whole, which is shorter than its diff:
```python
import jax
import jax.numpy as jnp
from jax import lax
from jax.sharding import PartitionSpec as P

SEQ_LEN = 2048


epsilon = 1e-05


def matmul(former, latter):
    return jnp.dot(former, latter, preferred_element_type=jnp.float32)


def matmul_nt(former, latter):
    return lax.dot_general(
        former, latter, (((1,), (1,)), ((), ())), preferred_element_type=jnp.float32
    )


def matmul_tn(former, latter):
    return lax.dot_general(
        former, latter, (((0,), (0,)), ((), ())), preferred_element_type=jnp.float32
    )


def rms_forward(values, norm_gain):
    inverse_rms = lax.rsqrt(jnp.mean(values * values, axis=-1, keepdims=True) + epsilon)
    return (values * inverse_rms * norm_gain, inverse_rms)


def rms_backward(values, inverse_rms, norm_gain, incoming):
    weighted = incoming * norm_gain
    normed = values * inverse_rms
    return inverse_rms * (
        weighted - normed * jnp.mean(weighted * normed, axis=-1, keepdims=True)
    )


def ring_pairs(axis):
    length = lax.axis_size(axis)
    return [(i, (i + 1) % length) for i in range(length)]


def ring_gather(block, axis):
    length = lax.axis_size(axis)
    me = lax.axis_index(axis)
    rows = block.shape[0]
    whole = jnp.zeros((length * rows, block.shape[1]), block.dtype)
    whole = lax.dynamic_update_slice(whole, block, (me * rows, 0))
    for step in range(1, length):
        block = lax.ppermute(block, axis, ring_pairs(axis))
        owner = (me - step + length) % length
        whole = lax.dynamic_update_slice(whole, block, (owner * rows, 0))
    return (whole, block)


def ring_scatter(terms, axis):
    length = lax.axis_size(axis)
    me = lax.axis_index(axis)
    rows = terms.shape[0] // length

    def own(step):
        block = (me - 1 - step + 2 * length) % length
        return lax.dynamic_slice(terms, (block * rows, 0), (rows, terms.shape[1]))

    total = own(0)
    for step in range(1, length):
        arrived = lax.ppermute(total.astype(jnp.bfloat16), axis, ring_pairs(axis))
        total = arrived.astype(jnp.float32) + own(step).astype(jnp.float32)
    return total.astype(jnp.float32)


def gather_rows(rows):
    return lax.all_gather(rows, "tensor", axis=0, tiled=True)


def scatter_rows(partial):
    return lax.psum_scatter(
        partial.astype(jnp.bfloat16), "tensor", scatter_dimension=0, tiled=True
    ).astype(jnp.float32)


def lagged(array, by):
    return jnp.pad(array, ((by, 0), (0, 0)))[: array.shape[0]]


def leading(array, by):
    return jnp.pad(array, ((0, by), (0, 0)))[by:]


def local(
    tokens,
    gain_one,
    in_weight,
    conv_weight,
    out_weight,
    gain_two,
    gate_weight,
    up_weight,
    down_weight,
    out_cotangent,
):
    width = tokens.shape[1]
    part = in_weight.shape[0]
    channels = in_weight.shape[2]
    units = gate_weight.shape[1]

    token_rows = tokens.astype(jnp.float32)
    normed_one, inverse_one = rms_forward(token_rows, gain_one)
    normed_all = gather_rows(normed_one.astype(jnp.bfloat16))
    cotangent_all = gather_rows(out_cotangent)

    mixer_part = jnp.concatenate(
        [in_weight.reshape(part, 3 * channels), out_weight.T], axis=1
    )
    mixer_full, last = ring_gather(mixer_part, "dp")
    in_full = mixer_full[:, : 3 * channels]
    out_turned = mixer_full[:, 3 * channels :]
    ffn_part = jnp.concatenate([gate_weight, up_weight, down_weight.T], axis=1)
    ffn_part, last = lax.optimization_barrier((ffn_part, last))
    ffn_full, _ = ring_gather(ffn_part, "dp")
    front_full = ffn_full[:, : 2 * units]
    down_turned = ffn_full[:, 2 * units :]

    channel_start = lax.axis_index("tensor") * channels
    taps = lax.dynamic_slice(conv_weight, (0, channel_start), (3, channels))
    row_count = normed_all.shape[0]
    positions = lax.broadcasted_iota(jnp.int32, (row_count, 1), 0) % SEQ_LEN

    projected = matmul(normed_all, in_full)
    gate_b = projected[:, :channels]
    gate_c = projected[:, channels : 2 * channels]
    values_x = projected[:, 2 * channels :]
    gated_input = gate_b * values_x
    lag_one = jnp.where(positions >= 1, lagged(gated_input, 1), 0.0)
    lag_two = jnp.where(positions >= 2, lagged(gated_input, 2), 0.0)
    convolved = taps[0] * gated_input + taps[1] * lag_one + taps[2] * lag_two
    mixer_low = (gate_c * convolved).astype(jnp.bfloat16)
    residual = token_rows + scatter_rows(matmul_nt(mixer_low, out_turned))

    normed_two, inverse_two = rms_forward(residual, gain_two)
    normed_two_all = gather_rows(normed_two.astype(jnp.bfloat16))

    front = matmul(normed_two_all, front_full)
    gate_act = front[:, :units]
    up_act = front[:, units:]
    grad_hidden = matmul(cotangent_all, down_turned)
    sigmoid_gate = jax.nn.sigmoid(gate_act)
    silu_gate = gate_act * sigmoid_gate
    hidden = (silu_gate * up_act).astype(jnp.bfloat16)
    grad_gate = (
        grad_hidden * up_act * sigmoid_gate * (1.0 + gate_act * (1.0 - sigmoid_gate))
    ).astype(jnp.bfloat16)
    grad_up = (grad_hidden * silu_gate).astype(jnp.bfloat16)
    grad_front = jnp.concatenate([grad_gate, grad_up], axis=1)
    grad_two = scatter_rows(matmul_nt(grad_front, front_full))
    block_out = (residual + scatter_rows(matmul_nt(hidden, down_turned))).astype(jnp.bfloat16)

    down_terms = matmul_tn(cotangent_all, hidden).astype(jnp.bfloat16)
    front_terms = matmul_tn(normed_two_all, grad_front)
    gain_two_grad = (
        jnp.sum(front_terms * front_full.astype(jnp.float32), axis=1) / gain_two
    )
    front_terms = front_terms.astype(jnp.bfloat16)
    down_grad = ring_scatter(down_terms, "dp")
    front_grad = ring_scatter(front_terms, "dp")

    grad_resid = out_cotangent.astype(jnp.float32) + rms_backward(
        residual, inverse_two, gain_two, grad_two
    )
    branch_all = gather_rows(grad_resid.astype(jnp.bfloat16))

    grad_mixer = matmul(branch_all, out_turned)
    out_terms = matmul_tn(branch_all, mixer_low)
    grad_conv = grad_mixer * gate_c
    lead_one = leading(jnp.where(positions >= 1, grad_conv, 0.0), 1)
    lead_two = leading(jnp.where(positions >= 2, grad_conv, 0.0), 2)
    grad_gated = taps[0] * grad_conv + taps[1] * lead_one + taps[2] * lead_two
    grad_proj = jnp.concatenate(
        [
            (grad_gated * values_x).astype(jnp.bfloat16),
            (grad_mixer * convolved).astype(jnp.bfloat16),
            (grad_gated * gate_b).astype(jnp.bfloat16),
        ],
        axis=1,
    )
    grad_one = scatter_rows(matmul_nt(grad_proj, in_full))
    in_terms = matmul_tn(normed_all, grad_proj)
    tap_grad = jnp.stack(
        [
            jnp.sum(grad_conv * gated_input, axis=0),
            jnp.sum(grad_conv * lag_one, axis=0),
            jnp.sum(grad_conv * lag_two, axis=0),
        ]
    )
    gain_one_grad = jnp.sum(in_terms * in_full.astype(jnp.float32), axis=1) / gain_one
    tap_full = lax.dynamic_update_slice(
        jnp.zeros((3, width), jnp.float32), tap_grad, (0, channel_start)
    )
    small = jnp.concatenate([gain_one_grad[None], gain_two_grad[None], tap_full], axis=0)
    small = lax.psum(small, ("dp", "tensor"))

    mixer_terms = jnp.concatenate(
        [in_terms.astype(jnp.bfloat16), out_terms.astype(jnp.bfloat16)], axis=1
    )
    mixer_grad = ring_scatter(mixer_terms, "dp")

    token_grad = grad_resid + rms_backward(token_rows, inverse_one, gain_one, grad_one)
    return (
        block_out,
        token_grad,
        small[0],
        mixer_grad[:, : 3 * channels].reshape(part, 3, channels),
        small[2:],
        mixer_grad[:, 3 * channels :].T,
        small[1],
        front_grad[:, :units],
        front_grad[:, units:],
        down_grad.T,
    )


def solution(mesh):
    return jax.shard_map(
        local,
        mesh=mesh,
        in_specs=(
            P(("dp", "tensor"), None),
            P(),
            P("dp", None, "tensor"),
            P(),
            P("tensor", "dp"),
            P(),
            P("dp", "tensor"),
            P("dp", "tensor"),
            P("tensor", "dp"),
            P(("dp", "tensor"), None),
        ),
        out_specs=(
            P(("dp", "tensor"), None),
            P(("dp", "tensor"), None),
            P(),
            P("dp", None, "tensor"),
            P(),
            P("tensor", "dp"),
            P(),
            P("dp", "tensor"),
            P("dp", "tensor"),
            P("tensor", "dp"),
        ),
        check_vma=False,
    )
```

time: 1180 us -> 625 us (0.53)
  waiting for transfers between devices: 885 us -> 367 us
  other arithmetic: 17.9 us -> 50.2 us
  local copies, waits for them, and re-layouts: 61 us -> 29.3 us
  matrix products: 133 us -> 111 us
  blocking collectives: 55.4 us -> 38.9 us
    all_gather x9 -> x4, waiting for transfers between devices: 465 us -> 53.1 us  [gather_rows(): return lax.all_gather(rows, 'tensor', axis=0, tiled=True)]
    unnamed x23 -> x8, waiting for transfers between devices: 225 us -> 0.14 us
    ppermute x2 -> x35, waiting for transfers between devices: 4.66 us -> 211 us  [the longest x14 140 us: ring_gather(): block = lax.ppermute(block, axis, ring_pairs(axis))]
    reduce_scatter x6 -> x4, waiting for transfers between devices: 190 us -> 102 us  [scatter_rows(): lax.psum_scatter(partial.astype(jnp.bfloat16), 'tensor', scatter_dimensio...]
    unnamed x62 -> x67, local copies, waits for them, and re-layouts: 49.2 us -> 8.95 us
    convert_element_type x8 -> x24, other arithmetic: 9.88 us -> 33.5 us  [the longest x18 20.2 us: ring_scatter(): arrived = lax.ppermute(total.astype(jnp.bfloat16), axis, ring_pairs(axis))]
    dot_general x5 -> x4, matrix products: 50.1 us -> 32.8 us  [matmul_nt(): lax.dot_general(former, latter, (((1,), (1,)), ((), ())), preferred_eleme...]
    all_gather x1 -> x0, blocking collectives: 14.8 us -> none  [local(): lax.all_gather(out_weight, 'dp', axis=1, tiled=True)]
  transfers between devices with their start and end apart: 21 -> 43, of which waited for: 18 -> 32; matrix products, arithmetic and copies ran while one was open for 14% -> 17% of each run, Pallas kernels for 0% -> 0%
where the time goes in v1:
time: 625 us; the launch traced here: 617 us
  waiting for transfers between devices  367 us (59%)
  matrix products  111 us (18%)
  other arithmetic  50.2 us (8%)
  blocking collectives  38.9 us (6%)
  local copies, waits for them, and re-layouts  29.3 us (5%)
  between operations  15.4 us (2%)
    ppermute x14, waiting for transfers between devices, ring_gather(): block = lax.ppermute(block, axis, ring_pairs(axis))  140 us
    reduce_scatter x4, waiting for transfers between devices, scatter_rows(): lax.psum_scatter(partial.astype(jnp.bfloat16), 'tensor', scatter_dimensio...  102 us
    ppermute x21, waiting for transfers between devices, ring_scatter(): arrived = lax.ppermute(total.astype(jnp.bfloat16), axis, ring_pairs(axis))  71.7 us
    all_gather x4, waiting for transfers between devices, gather_rows(): return lax.all_gather(rows, 'tensor', axis=0, tiled=True)  53.1 us
    dot_general x4, matrix products, matmul(): return jnp.dot(former, latter, preferred_element_type=jnp.float32)  46.1 us
    psum x1, blocking collectives, local(): small = lax.psum(small, ('dp', 'tensor'))  38.9 us
    dot_general x4, matrix products, matmul_nt(): lax.dot_general(former, latter, (((1,), (1,)), ((), ())), preferred_eleme...  32.8 us
    dot_general x4, matrix products, matmul_tn(): lax.dot_general(former, latter, (((0,), (0,)), ((), ())), preferred_eleme...  32.4 us
  transfers between devices with their start and end apart: 43, of which 32 were waited for; matrix products, arithmetic and copies ran while one was open for 17% of the time, Pallas kernels for 0%

profile of v1, /device:TPU:0, one launch (start us, length us, event | category | flops | bytes accessed | tf_op | source)
XLA Modules:
  0.0 617.4 jit_solution(17055351291037458002)
XLA Ops:
  12.7 8.1 %collective-permute-done = bf16[128,1024]{0,1:T(8,128)(2,1)S(1)} collective-permute-done((bf16[128,1024]{0,1:T(8,128)(2,1)S(1)}, bf16[128,1024]{0,1:T(8,128)(2,1)S(1)}, u32[]{:S(2)}, u32[]{:S(2)}) %collective-permute-start) | collective-permute-done | bytes 262176 | tf_op jit(solution)/shard_map/ppermute | solution.py:53
  20.8 7.6 %collective-permute-done.1 = bf16[128,1024]{0,1:T(8,128)(2,1)S(1)} collective-permute-done((bf16[128,1024]{0,1:T(8,128)(2,1)S(1)}, bf16[128,1024]{0,1:T(8,128)(2,1)S(1)}, u32[]{:S(2)}, u32[]{:S(2)}) %collective-permute-start.1) | collective-permute-done | bytes 262176 | tf_op jit(solution)/shard_map/ppermute | solution.py:53
  28.4 7.6 %collective-permute-done.2 = bf16[128,1024]{0,1:T(8,128)(2,1)S(1)} collective-permute-done((bf16[128,1024]{0,1:T(8,128)(2,1)S(1)}, bf16[128,1024]{0,1:T(8,128)(2,1)S(1)}, u32[]{:S(2)}, u32[]{:S(2)}) %collective-permute-start.2) | collective-permute-done | bytes 262176 | tf_op jit(solution)/shard_map/ppermute | solution.py:53
  36.0 7.6 %collective-permute-done.3 = bf16[128,1024]{0,1:T(8,128)(2,1)S(1)} collective-permute-done((bf16[128,1024]{0,1:T(8,128)(2,1)S(1)}, bf16[128,1024]{0,1:T(8,128)(2,1)S(1)}, u32[]{:S(2)}, u32[]{:S(2)}) %collective-permute-start.3) | collective-permute-done | bytes 262176 | tf_op jit(solution)/shard_map/ppermute | solution.py:53
  81.3 52.4 %reduce-scatter.5.cloned.1.call-done = bf16[512,1024]{1,0:T(8,128)(2,1)} async-done(((bf16[2048,1024]{1,0:T(8,128)(2,1)}), bf16[512,1024]{1,0:T(8,128)(2,1)}) %reduce-scatter.5.cloned.1.call-update) | async-done | bytes 1048592 | tf_op jit(solution)/shard_map/reduce_scatter | solution.py:80
  138.4 14.3 %collective-permute-done.7 = bf16[128,3456]{1,0:T(8,128)(2,1)S(1)} collective-permute-done((bf16[128,3456]{1,0:T(8,128)(2,1)S(1)}, bf16[128,3456]{1,0:T(8,128)(2,1)S(1)}, u32[]{:S(2)}, u32[]{:S(2)}) %collective-permute-start.7) | collective-permute-done | bytes 884768 | tf_op jit(solution)/shard_map/ppermute | solution.py:53
  153.6 14.4 %collective-permute-done.8 = bf16[128,3456]{1,0:T(8,128)(2,1)} collective-permute-done((bf16[128,3456]{1,0:T(8,128)(2,1)S(1)}, bf16[128,3456]{1,0:T(8,128)(2,1)}, u32[]{:S(2)}, u32[]{:S(2)}) %collective-permute-start.8) | collective-permute-done | bytes 884768 | tf_op jit(solution)/shard_map/ppermute | solution.py:53
  168.0 14.5 %collective-permute-done.9 = bf16[128,3456]{1,0:T(8,128)(2,1)} collective-permute-done((bf16[128,3456]{1,0:T(8,128)(2,1)}, bf16[128,3456]{1,0:T(8,128)(2,1)}, u32[]{:S(2)}, u32[]{:S(2)}) %collective-permute-start.9) | collective-permute-done | bytes 884768 | tf_op jit(solution)/shard_map/ppermute | solution.py:53
  186.9 10.1 %collective-permute-done.10 = bf16[128,3456]{1,0:T(8,128)(2,1)S(1)} collective-permute-done((bf16[128,3456]{1,0:T(8,128)(2,1)}, bf16[128,3456]{1,0:T(8,128)(2,1)S(1)}, u32[]{:S(2)}, u32[]{:S(2)}) %collective-permute-start.10) | collective-permute-done | bytes 884768 | tf_op jit(solution)/shard_map/ppermute | solution.py:53
  200.3 11.0 %collective-permute-done.11 = bf16[128,3456]{1,0:T(8,128)(2,1)S(1)} collective-permute-done((bf16[128,3456]{1,0:T(8,128)(2,1)S(1)}, bf16[128,3456]{1,0:T(8,128)(2,1)S(1)}, u32[]{:S(2)}, u32[]{:S(2)}) %collective-permute-start.11) | collective-permute-done | bytes 884768 | tf_op jit(solution)/shard_map/ppermute | solution.py:53
  214.4 11.1 %collective-permute-done.12 = bf16[128,3456]{1,0:T(8,128)(2,1)S(1)} collective-permute-done((bf16[128,3456]{1,0:T(8,128)(2,1)S(1)}, bf16[128,3456]{1,0:T(8,128)(2,1)S(1)}, u32[]{:S(2)}, u32[]{:S(2)}) %collective-permute-start.12) | collective-permute-done | bytes 884768 | tf_op jit(solution)/shard_map/ppermute | solution.py:53
  228.0 12.2 %collective-permute-done.13 = bf16[128,3456]{1,0:T(8,128)(2,1)S(1)} collective-permute-done((bf16[128,3456]{1,0:T(8,128)(2,1)S(1)}, bf16[128,3456]{1,0:T(8,128)(2,1)S(1)}, u32[]{:S(2)}, u32[]{:S(2)}) %collective-permute-start.13) | collective-permute-done | bytes 884768 | tf_op jit(solution)/shard_map/ppermute | solution.py:53
  241.3 16.7 %fusion.9 = f32[2048,2304]{1,0:T(8,128)} fusion(bf16[2048,1024]{1,0:T(8,128)(2,1)} %all-gather.7.cloned.1.call-done, bf16[1024,3456]{1,0:T(8,128)(2,1)} %constant_dynamic-update-slice_fusion.1), kind=kOutput, calls=%fused_computation.27 | convolution fusion | flops 9663676416 | bytes 27787264 | tf_op jit(solution)/shard_map/dot_general | solution.py:13
  258.0 17.1 %fusion.2 = (bf16[2048,1152]{1,0:T(8,128)(2,1)S(1)}, bf16[2048,1152]{1,0:T(8,128)(2,1)}, bf16[2048,1152]{1,0:T(8,128)(2,1)}) fusion(f32[2048,2304]{1,0:T(8,128)} %fusion.9, bf16[2048,1024]{1,0:T(8,128)(2,1)} %all-gather.9.cloned.1.call-done, bf16[1024,3456]{1,0:T(8,128)(2,1)} %constant_dynamic-update-slice_fusion.1), kind=kOutput, calls=%fused_computation.5 | convolution fusion | flops 4867227648 | bytes 39583744 | tf_op jit(solution)/shard_map/dot_general | solution.py:13
  277.2 14.6 %fusion.7 = bf16[2048,1024]{1,0:T(8,128)(2,1)} fusion(bf16[2048,1152]{1,0:T(8,128)(2,1)} %get-tuple-element.31, bf16[2048,1152]{1,0:T(8,128)(2,1)S(1)} %get-tuple-element.30, bf16[1024,3456]{1,0:T(8,128)(2,1)} %constant_dynamic-update-slice_fusion.1), kind=kOutput, calls=%fused_computation.21 | convolution fusion | flops 9684647936 | bytes 18350080 | tf_op jit(solution)/shard_map/dot_general | solution.py:17
  292.0 49.8 %reduce-scatter.9.cloned.1.call-done = bf16[512,1024]{1,0:T(8,128)(2,1)} async-done(((bf16[2048,1024]{1,0:T(8,128)(2,1)}), bf16[512,1024]{1,0:T(8,128)(2,1)}) %reduce-scatter.9.cloned.1.call-update) | async-done | bytes 1048592 | tf_op jit(solution)/shard_map/reduce_scatter | solution.py:80
  345.8 52.8 %all-gather.11.cloned.1.call-done = bf16[2048,1024]{1,0:T(8,128)(2,1)} async-done(((bf16[512,1024]{1,0:T(8,128)(2,1)}), bf16[2048,1024]{1,0:T(8,128)(2,1)}) %all-gather.11.cloned.1.call-update) | async-done | bytes 4194320 | tf_op jit(solution)/shard_map/all_gather | solution.py:76
  416.9 8.5 %convolution_convert_fusion = bf16[1152,1024]{1,0:T(8,128)(2,1)S(1)} fusion(bf16[2048,1152]{1,0:T(8,128)(2,1)} %get-tuple-element.32, bf16[2048,1024]{1,0:T(8,128)(2,1)} %all-gather.9.cloned.1.call-done), kind=kOutput, calls=%fused_computation.22 | convolution fusion | flops 4833017856 | bytes 11272192 | tf_op jit(solution)/shard_map/dot_general | solution.py:23
  425.8 15.8 %fusion.63 = (bf16[1024,2304]{1,0:T(8,128)(2,1)S(1)}, f32[1024]{0:T(1024)S(1)}) fusion(bf16[1024,3456]{1,0:T(8,128)(2,1)} %constant_dynamic-update-slice_fusion.1, bf16[2048,1024]{1,0:T(8,128)(2,1)S(1)} %copy-done.29, bf16[2048,1152]{1,0:T(8,128)(2,1)} %get-tuple-element.31, bf16[2048,1152]{1,0:T(8,128)(2,1)} %copy-done.31), kind=kOutput, calls=%fused_computation.168 | convolution fusion | flops 9691986944 | bytes 23072768 | tf_op jit(solution)/shard_map/dot_general | solution.py:23
  462.6 8.1 %collective-permute-done.22 = bf16[128,2304]{1,0:T(8,128)(2,1)} collective-permute-done((bf16[128,2304]{1,0:T(8,128)(2,1)}, bf16[128,2304]{1,0:T(8,128)(2,1)}, u32[]{:S(2)}, u32[]{:S(2)}) %collective-permute-start.22) | collective-permute-done | bytes 589856 | tf_op jit(solution)/shard_map/ppermute | solution.py:70
  475.7 8.7 %collective-permute-done.23 = bf16[128,2304]{1,0:T(8,128)(2,1)} collective-permute-done((bf16[128,2304]{1,0:T(8,128)(2,1)}, bf16[128,2304]{1,0:T(8,128)(2,1)}, u32[]{:S(2)}, u32[]{:S(2)}) %collective-permute-start.23) | collective-permute-done | bytes 589856 | tf_op jit(solution)/shard_map/ppermute | solution.py:70
  486.5 10.0 %convolution_convert_fusion.1 = bf16[2048,1024]{1,0:T(8,128)(2,1)} fusion(bf16[2048,1152]{1,0:T(8,128)(2,1)} %get-tuple-element.32, bf16[1024,3456]{1,0:T(8,128)(2,1)} %constant_dynamic-update-slice_fusion.1), kind=kOutput, calls=%fused_computation.23 | convolution fusion | flops 4833935360 | bytes 11272192 | tf_op jit(solution)/shard_map/dot_general | solution.py:17
  516.9 10.4 %collective-permute-done.15 = bf16[128,1024]{0,1:T(8,128)(2,1)S(1)} collective-permute-done((bf16[128,1024]{0,1:T(8,128)(2,1)S(1)}, bf16[128,1024]{0,1:T(8,128)(2,1)S(1)}, u32[]{:S(2)}, u32[]{:S(2)}) %collective-permute-start.15) | collective-permute-done | bytes 262176 | tf_op jit(solution)/shard_map/ppermute | solution.py:70
  560.5 38.9 %psum.7 = f32[5,1024]{1,0:T(8,128)S(1)} all-reduce(f32[5,1024]{1,0:T(8,128)S(1)} %pad_maximum_fusion.10), channel_id=1, replica_groups=mesh['dp'=8,'tensor'=4] {'dp','tensor'}, use_global_device_ids=true, to_apply=%region_13.14 | all-reduce | flops 5120 | bytes 40960 | tf_op jit(solution)/shard_map/psum | solution.py:203
  (222 shorter events, 179.9 us)
Async XLA Ops:
  7.2 59.7 %all-gather.5.cloned.1.call-start = ((), (), s32[]{:S(2)}) async-start(), calls=%async_computation.4 | async-start | bytes 5242880 | tf_op jit(solution)/shard_map/all_gather | solution.py:76
  11.3 122.4 %reduce-scatter.5.cloned.1.call-start = ((), (), s32[]{:S(2)}) async-start(), calls=%async_computation.5 | async-start | bytes 5242880 | tf_op jit(solution)/shard_map/reduce_scatter | solution.py:80
  81.3 160.0 %all-gather.7.cloned.1.call-start = ((), (), s32[]{:S(2)}) async-start(), calls=%async_computation.6 | async-start | bytes 5242880 | tf_op jit(solution)/shard_map/all_gather | solution.py:76
  136.9 121.0 %all-gather.9.cloned.1.call-start = ((), (), s32[]{:S(2)}) async-start(), calls=%async_computation.8 | async-start | bytes 5242880 | tf_op jit(solution)/shard_map/all_gather | solution.py:76
  138.3 14.3 %collective-permute-start.7 = (bf16[128,3456]{1,0:T(8,128)(2,1)S(1)}, bf16[128,3456]{1,0:T(8,128)(2,1)S(1)}, u32[]{:S(2)}, u32[]{:S(2)}) collective-permute-start(bf16[128,3456]{1,0:T(8,128)(2,1)S(1)} %pad_maximum_fusion.8), channel_id=1, source_target_pairs={{0,4},{4,8},{8,12},{12,16},{16,20},{20,24},{24,28},{28,0},{1,5},{5... | collective-permute-start | bytes 2654216 | tf_op jit(solution)/shard_map/ppermute | solution.py:53
  153.6 14.4 %collective-permute-start.8 = (bf16[128,3456]{1,0:T(8,128)(2,1)S(1)}, bf16[128,3456]{1,0:T(8,128)(2,1)}, u32[]{:S(2)}, u32[]{:S(2)}) collective-permute-start(bf16[128,3456]{1,0:T(8,128)(2,1)S(1)} %collective-permute-done.7), channel_id=1, source_target_pairs={{0,4},{4,8},{8,12},{12,16},{16,20},{20,24},{24,28},{28,0},{1,5},{5... | collective-permute-start | bytes 2654216 | tf_op jit(solution)/shard_map/ppermute | solution.py:53
  167.9 14.6 %collective-permute-start.9 = (bf16[128,3456]{1,0:T(8,128)(2,1)}, bf16[128,3456]{1,0:T(8,128)(2,1)}, u32[]{:S(2)}, u32[]{:S(2)}) collective-permute-start(bf16[128,3456]{1,0:T(8,128)(2,1)} %collective-permute-done.8), channel_id=1, source_target_pairs={{0,4},{4,8},{8,12},{12,16},{16,20},{20,24},{24,28},{28,0},{1,5},{5... | collective-permute-start | bytes 2654216 | tf_op jit(solution)/shard_map/ppermute | solution.py:53
  168.0 173.9 %reduce-scatter.9.cloned.1.call-start = ((), (), s32[]{:S(2)}) async-start(), calls=%async_computation.9 | async-start | bytes 5242880 | tf_op jit(solution)/shard_map/reduce_scatter | solution.py:80
  182.5 14.5 %collective-permute-start.10 = (bf16[128,3456]{1,0:T(8,128)(2,1)}, bf16[128,3456]{1,0:T(8,128)(2,1)S(1)}, u32[]{:S(2)}, u32[]{:S(2)}) collective-permute-start(bf16[128,3456]{1,0:T(8,128)(2,1)} %collective-permute-done.9), channel_id=1, source_target_pairs={{0,4},{4,8},{8,12},{12,16},{16,20},{20,24},{24,28},{28,0},{1,5},{5... | collective-permute-start | bytes 2654216 | tf_op jit(solution)/shard_map/ppermute | solution.py:53
  197.0 14.3 %collective-permute-start.11 = (bf16[128,3456]{1,0:T(8,128)(2,1)S(1)}, bf16[128,3456]{1,0:T(8,128)(2,1)S(1)}, u32[]{:S(2)}, u32[]{:S(2)}) collective-permute-start(bf16[128,3456]{1,0:T(8,128)(2,1)S(1)} %collective-permute-done.10), channel_id=1, source_target_pairs={{0,4},{4,8},{8,12},{12,16},{16,20},{20,24},{24,28},{28,0},{1,5},{5... | collective-permute-start | bytes 2654216 | tf_op jit(solution)/shard_map/ppermute | solution.py:53
  211.3 14.3 %collective-permute-start.12 = (bf16[128,3456]{1,0:T(8,128)(2,1)S(1)}, bf16[128,3456]{1,0:T(8,128)(2,1)S(1)}, u32[]{:S(2)}, u32[]{:S(2)}) collective-permute-start(bf16[128,3456]{1,0:T(8,128)(2,1)S(1)} %collective-permute-done.11), channel_id=1, source_target_pairs={{0,4},{4,8},{8,12},{12,16},{16,20},{20,24},{24,28},{28,0},{1,5},{5... | collective-permute-start | bytes 2654216 | tf_op jit(solution)/shard_map/ppermute | solution.py:53
  225.6 14.7 %collective-permute-start.13 = (bf16[128,3456]{1,0:T(8,128)(2,1)S(1)}, bf16[128,3456]{1,0:T(8,128)(2,1)S(1)}, u32[]{:S(2)}, u32[]{:S(2)}) collective-permute-start(bf16[128,3456]{1,0:T(8,128)(2,1)S(1)} %collective-permute-done.12), channel_id=1, source_target_pairs={{0,4},{4,8},{8,12},{12,16},{16,20},{20,24},{24,28},{28,0},{1,5},{5... | collective-permute-start | bytes 2654216 | tf_op jit(solution)/shard_map/ppermute | solution.py:53
  291.8 106.7 %all-gather.11.cloned.1.call-start = ((), (), s32[]{:S(2)}) async-start(), calls=%async_computation.10 | async-start | bytes 5242880 | tf_op jit(solution)/shard_map/all_gather | solution.py:76
  345.7 258.4 %reduce-scatter.11.cloned.1.call-start = ((), (), s32[]{:S(2)}) async-start(), calls=%async_computation.11 | async-start | bytes 5242880 | tf_op jit(solution)/shard_map/reduce_scatter | solution.py:80
  416.8 189.0 %reduce-scatter.7.cloned.1.call-start = ((), (), s32[]{:S(2)}) async-start(), calls=%async_computation.7 | async-start | bytes 5242880 | tf_op jit(solution)/shard_map/reduce_scatter | solution.py:80
  425.5 16.1 %collective-permute-start.28 = (bf16[128,1152]{0,1:T(8,128)(2,1)S(1)}, bf16[128,1152]{0,1:T(8,128)(2,1)S(1)}, u32[]{:S(2)}, u32[]{:S(2)}) collective-permute-start(bf16[128,1152]{0,1:T(8,128)(2,1)S(1)} %dynamic-slice_bitcast_fusion), channel_id=1, source_target_pairs={{0,4},{4,8},{8,12},{12,16},{16,20},{20,24},{24,28},{28,0},{1,5},{5... | collective-permute-start | bytes 884744 | tf_op jit(solution)/shard_map/ppermute | solution.py:70
  444.7 12.4 %collective-permute-start.21 = (bf16[128,2304]{1,0:T(8,128)(2,1)}, bf16[128,2304]{1,0:T(8,128)(2,1)}, u32[]{:S(2)}, u32[]{:S(2)}) collective-permute-start(bf16[128,2304]{1,0:T(8,128)(2,1)} %constant_dynamic-slice_fusion.1), channel_id=1, source_target_pairs={{0,4},{4,8},{8,12},{12,16},{16,20},{20,24},{24,28},{28,0},{1,5},{5... | collective-permute-start | bytes 1769480 | tf_op jit(solution)/shard_map/ppermute | solution.py:70
  475.6 20.9 %collective-permute-start.32 = (bf16[128,1152]{0,1:T(8,128)(2,1)}, bf16[128,1152]{0,1:T(8,128)(2,1)}, u32[]{:S(2)}, u32[]{:S(2)}) collective-permute-start(bf16[128,1152]{0,1:T(8,128)(2,1)} %fusion.37), channel_id=1, source_target_pairs={{0,4},{4,8},{8,12},{12,16},{16,20},{20,24},{24,28},{28,0},{1,5},{5... | collective-permute-start | bytes 884744 | tf_op jit(solution)/shard_map/ppermute | solution.py:70
  497.8 18.0 %collective-permute-start.33 = (bf16[128,1152]{0,1:T(8,128)(2,1)S(1)}, bf16[128,1152]{0,1:T(8,128)(2,1)S(1)}, u32[]{:S(2)}, u32[]{:S(2)}) collective-permute-start(bf16[128,1152]{0,1:T(8,128)(2,1)S(1)} %fusion.36), channel_id=1, source_target_pairs={{0,4},{4,8},{8,12},{12,16},{16,20},{20,24},{24,28},{28,0},{1,5},{5... | collective-permute-start | bytes 884744 | tf_op jit(solution)/shard_map/ppermute | solution.py:70
  499.3 12.7 %collective-permute-start.25 = (bf16[128,2304]{1,0:T(8,128)(2,1)S(1)}, bf16[128,2304]{1,0:T(8,128)(2,1)S(1)}, u32[]{:S(2)}, u32[]{:S(2)}) collective-permute-start(bf16[128,2304]{1,0:T(8,128)(2,1)S(1)} %add_convert_fusion.3), channel_id=1, source_target_pairs={{0,4},{4,8},{8,12},{12,16},{16,20},{20,24},{24,28},{28,0},{1,5},{5... | collective-permute-start | bytes 1769480 | tf_op jit(solution)/shard_map/ppermute | solution.py:70
  513.4 14.1 %collective-permute-start.26 = (bf16[128,2304]{1,0:T(8,128)(2,1)S(1)}, bf16[128,2304]{1,0:T(8,128)(2,1)S(1)}, u32[]{:S(2)}, u32[]{:S(2)}) collective-permute-start(bf16[128,2304]{1,0:T(8,128)(2,1)S(1)} %add_convert_fusion.2), channel_id=1, source_target_pairs={{0,4},{4,8},{8,12},{12,16},{16,20},{20,24},{24,28},{28,0},{1,5},{5... | collective-permute-start | bytes 1769480 | tf_op jit(solution)/shard_map/ppermute | solution.py:70
  516.9 18.4 %collective-permute-start.34 = (bf16[128,1152]{0,1:T(8,128)(2,1)S(1)}, bf16[128,1152]{0,1:T(8,128)(2,1)S(1)}, u32[]{:S(2)}, u32[]{:S(2)}) collective-permute-start(bf16[128,1152]{0,1:T(8,128)(2,1)S(1)} %fusion.35), channel_id=1, source_target_pairs={{0,4},{4,8},{8,12},{12,16},{16,20},{20,24},{24,28},{28,0},{1,5},{5... | collective-permute-start | bytes 884744 | tf_op jit(solution)/shard_map/ppermute | solution.py:70
  528.7 15.6 %collective-permute-start.27 = (bf16[128,2304]{1,0:T(8,128)(2,1)S(1)}, bf16[128,2304]{1,0:T(8,128)(2,1)S(1)}, u32[]{:S(2)}, u32[]{:S(2)}) collective-permute-start(bf16[128,2304]{1,0:T(8,128)(2,1)S(1)} %add_convert_fusion.1), channel_id=1, source_target_pairs={{0,4},{4,8},{8,12},{12,16},{16,20},{20,24},{24,28},{28,0},{1,5},{5... | collective-permute-start | bytes 1769480 | tf_op jit(solution)/shard_map/ppermute | solution.py:70
  560.4 40.2 %collective-permute-start.20 = (bf16[128,1024]{0,1:T(8,128)(2,1)}, bf16[128,1024]{0,1:T(8,128)(2,1)S(1)}, u32[]{:S(2)}, u32[]{:S(2)}) collective-permute-start(bf16[128,1024]{0,1:T(8,128)(2,1)} %add_convert_fusion.7), channel_id=1, source_target_pairs={{0,4},{4,8},{8,12},{12,16},{16,20},{20,24},{24,28},{28,0},{1,5},{5... | collective-permute-start | bytes 786440 | tf_op jit(solution)/shard_map/ppermute | solution.py:70
  (51 other events, 510.0 us)
Sparse Core Ops, SparseCore 0:
  11.4 55.3 all-gather.4
  81.4 52.3 reduce-scatter.4
  137.0 52.6 all-gather.6
  191.6 52.6 all-gather.8
  291.9 49.8 reduce-scatter.8
  345.8 52.6 all-gather.10
  417.0 52.6 reduce-scatter.10
  496.6 53.0 reduce-scatter.6
